TPU v7x, 512 devices: a whole 4x4x16 slice. The times are simulated.
512 devices in a mesh: flop: 64 (over z, y), turn: 8 (over x, core).
Axes of the slice: x: 4, y: 4, z: 16, core: 2. Of those that a mesh axis runs over, the one named last changes fastest.
Arguments:
- root_reach: float32 [2, 1326], replicated, may hold values from 0.05 to 1
- stakes: float32 [5, 5], replicated, may hold values from 0.005 to 0.05
- flop_regrets: float32 [64, 5, 1326], P('flop'), may hold values from 0.1 to 1
- turn_regrets: float32 [64, 5, 32, 5, 1326], P('flop', None, 'turn'), may hold values from 0.1 to 1
- flop_cards: int32 [64, 3], P('flop'), may hold values from 0 to 51, as said below
- turn_cards: int32 [64, 32], P('flop', 'turn'), may hold values from 0 to 51, as said below
- river_cards: int32 [64, 32, 8], P('flop', 'turn'), may hold values from 0 to 51, as said below
- hand_ranks: int32 [64, 32, 8, 1326], P('flop', 'turn'), may hold values from 0 to 7461
- board_count: int32 [64, 8], P('flop', 'turn'), may hold values from 8 to 32, as said below
Outputs:
- flop_next: float32 [64, 5, 1326], P('flop')
- turn_next: float32 [64, 5, 32, 5, 1326], P('flop', None, 'turn')
- root_values: float32 [2, 1326], replicated
Inputs may be any that keep to these rules, and one draw needn't show every extreme that they name: `flop_cards`: for each flop, its three flop cards, its 32 turn cards and the 8 river cards of any one of its turn cards are all different cards. `turn_cards`: different cards within one flop, none of them a flop card of that flop. `river_cards`: the 8 river cards of one turn card differ from each other, from that turn card and from the flop's cards. board_count[f, g] + board_count[(f + 32) mod 64, g] = 40 for every f and g.
All inputs are finite; a program needn't handle non-finite values.
Results may differ from a plain program's by a relative error of at most 0.0003.
Values may be sent and summed in bfloat16 or wider, within the bound.
No kernel may reach another device: no remote copies, remote signals or barrier semaphores. Data moves between devices by JAX's collectives and lax.ppermute only.
A program may use at most 64 MiB of HBM per device.

v0:
```python
import jax
import jax.numpy as jnp
import numpy as np
from jax import lax
from jax.sharding import PartitionSpec as P

digit_base = 64


def swapped(block, axis, bit):
    count = lax.axis_size(axis)
    route = []
    for low in range(count):
        high = low | 1 << bit
        if high != low and high < count:
            route += [(low, high), (high, low)]
    return lax.ppermute(block, axis, route)


def hand_tables():
    low_np, high_np = np.triu_indices(52, 1)
    return (jnp.asarray(low_np.astype(np.int32)), jnp.asarray(high_np.astype(np.int32)))


def avoiding(low_card, high_card, cards):
    picked = cards[..., None]
    return ((low_card != picked) & (high_card != picked)).astype(jnp.float32)


def showdown(board_items, low_card, high_card, actions):
    hands = low_card.shape[0]
    width = 2 * actions
    halfway = hands // 2

    def board_sums(board_item):
        columns = board_item[:width]
        ranking = board_item[width].astype(jnp.float32) * digit_base + board_item[width + 1].astype(
            jnp.float32
        )
        pieces = []
        for section in range(2):
            rows = slice(section * halfway, (section + 1) * halfway)
            row_low = low_card[rows][:, None]
            row_high = high_card[rows][:, None]
            sharing = (row_low == low_card[None, :]) | (row_low == high_card[None, :])
            sharing = sharing | (row_high == low_card[None, :]) | (row_high == high_card[None, :])
            table = jnp.where(
                sharing, 0.0, jnp.sign(ranking[rows][:, None] - ranking[None, :])
            ).astype(jnp.bfloat16)
            pieces.append(
                lax.dot_general(
                    columns, table, (((1,), (1,)), ((), ())), preferred_element_type=jnp.float32
                )
            )
        product = jnp.concatenate(pieces, axis=1)
        return jnp.concatenate([product[actions:], product[:actions]], axis=0)

    return lax.map(board_sums, board_items)


def per_device(
    root_reach,
    stakes,
    flop_regrets,
    turn_regrets,
    flop_cards,
    turn_cards,
    river_cards,
    hand_ranks,
    board_count,
):
    low_card, high_card = hand_tables()
    actions = flop_regrets.shape[1]
    hands = flop_regrets.shape[2]
    turns_here = turn_cards.shape[1]
    rivers = river_cards.shape[2]
    capacity = turns_here * rivers
    surplus = capacity * 3 // 8
    balanced = capacity - surplus
    turns_all = turns_here * lax.axis_size("turn")
    flop_board = flop_cards[0]
    flop_mask = (
        avoiding(low_card, high_card, flop_board[0])
        * avoiding(low_card, high_card, flop_board[1])
        * avoiding(low_card, high_card, flop_board[2])
    )
    turn_mask = avoiding(low_card, high_card, turn_cards[0])
    river_mask = avoiding(low_card, high_card, river_cards[0])
    flop_policy = flop_regrets[0] / jnp.sum(flop_regrets[0], axis=0, keepdims=True)
    turn_policy = turn_regrets[0] / jnp.sum(turn_regrets[0], axis=2, keepdims=True)
    live_count = board_count[0, 0]
    live = (
        (jnp.arange(capacity, dtype=jnp.int32) < live_count)
        .astype(jnp.float32)
        .reshape(turns_here, rivers)
    )
    reach_zero = root_reach[0] * flop_mask
    reach_one = root_reach[1] * flop_mask
    zero_cols = (
        (reach_zero[None, :] * flop_policy)[None, None]
        * turn_mask[:, None, None, :]
        * river_mask[:, :, None, :]
    ).astype(jnp.bfloat16)
    one_base = reach_one[None, :] * turn_mask
    one_prod = one_base[None, :, None, :] * turn_policy
    one_mix = jnp.transpose(jnp.sum(stakes[:, None, :, None] * one_prod, axis=2), (1, 0, 2))
    one_cols = (one_mix[:, None] * river_mask[:, :, None, :]).astype(jnp.bfloat16)
    rank_high = (hand_ranks[0] // digit_base).astype(jnp.bfloat16)
    rank_low = (hand_ranks[0] % digit_base).astype(jnp.bfloat16)
    board_items = jnp.concatenate(
        [zero_cols, one_cols, rank_high[:, :, None], rank_low[:, :, None]], axis=2
    )
    board_items = board_items.reshape(capacity, 2 * actions + 2, hands)
    pair_bit = lax.axis_size("flop").bit_length() - 2
    arrived = swapped(board_items[balanced:], "flop", pair_bit)
    offsets = jnp.arange(balanced, dtype=jnp.int32) - live_count
    taken = jnp.take(arrived, jnp.clip(offsets, 0, surplus - 1), axis=0)
    merged = jnp.where((offsets >= 0)[:, None, None], taken, board_items[:balanced])
    results = showdown(merged, low_card, high_card, actions)
    back_index = jnp.arange(surplus, dtype=jnp.int32) + live_count
    outgoing = jnp.take(results, jnp.clip(back_index, 0, balanced - 1), axis=0)
    outgoing = jnp.where((back_index < balanced)[:, None, None], outgoing, 0.0)
    returned = swapped(outgoing, "flop", pair_bit)
    all_results = jnp.concatenate([results, returned], axis=0)
    all_results = all_results.reshape(turns_here, rivers, 2 * actions, hands)
    weight = flop_mask[None, None, :] * turn_mask[:, None, :] * river_mask * live[:, :, None]
    zero_turn = jnp.sum(all_results[:, :, :actions] * weight[:, :, None, :], axis=1) / rivers
    one_mean = jnp.sum(all_results[:, :, actions:] * weight[:, :, None, :], axis=1) / rivers
    one_action = stakes[:, None, :, None] * jnp.transpose(one_mean, (1, 0, 2))[:, :, None, :]
    one_turn = jnp.sum(turn_policy * one_action, axis=2)
    turn_next = jnp.maximum(turn_regrets[0] + one_action - one_turn[:, :, None, :], 0.0)[None]
    zero_share = jnp.sum(zero_turn, axis=0) / turns_all
    one_share = jnp.sum(one_turn, axis=(0, 1)) / turns_all
    zero_action, one_flop = lax.psum((zero_share, one_share), "turn")
    zero_flop = jnp.sum(flop_policy * zero_action, axis=0)
    flop_next = jnp.maximum(flop_regrets[0] + zero_action - zero_flop, 0.0)[None]
    root_zero, root_one = lax.psum((zero_flop, one_flop), "flop")
    root_values = jnp.stack([root_zero, root_one])
    return (flop_next, turn_next, root_values)


def solution(mesh):
    in_specs = (
        P(),
        P(),
        P("flop", None, None),
        P("flop", None, "turn", None, None),
        P("flop", None),
        P("flop", "turn"),
        P("flop", "turn", None),
        P("flop", "turn", None, None),
        P("flop", "turn"),
    )
    out_specs = (P("flop", None, None), P("flop", None, "turn", None, None), P())
    return jax.shard_map(
        per_device, mesh=mesh, in_specs=in_specs, out_specs=out_specs, check_vma=False
    )
```

profile of v0, /device:TPU:2, one launch (start us, length us, event | category | flops | bytes accessed | tf_op | source)
XLA Modules:
  0.0 604.8 jit_solution(14226353872796064874)
XLA Ops:
  13.6 15.7 %collective-permute-start = (bf16[12,12,1326]{2,1,0:T(8,128)(2,1)}, bf16[12,12,1326]{2,1,0:T(8,128)(2,1)}, u32[]{:S(2)}, u32[]{:S(2)}) collective-permute-start(bf16[12,12,1326]{2,1,0:T(8,128)(2,1)} %pad_maximum_fusion.5), channel_id=1, source_target_pairs={{0,256},{256,0},{8,264},{264,8},{16,272},{272,16},{24,280},{280,24... | collective-permute-start | bytes 1145672 | tf_op jit(solution)/shard_map/ppermute | solution.py:17
  30.1 16.4 %collective-permute-done = bf16[12,12,1326]{2,1,0:T(8,128)(2,1)} collective-permute-done((bf16[12,12,1326]{2,1,0:T(8,128)(2,1)}, bf16[12,12,1326]{2,1,0:T(8,128)(2,1)}, u32[]{:S(2)}, u32[]{:S(2)}) %collective-permute-start) | collective-permute-done | bytes 381920 | tf_op jit(solution)/shard_map/ppermute | solution.py:17
  49.1 3.2 fusion.20
  52.4 145.3 %while.11 = (s32[]{:T(128)}, f32[20,10,1326]{2,1,0:T(8,128)S(1)}, bf16[20,12,1326]{2,1,0:T(8,128)(2,1)}, s32[]{:T(128)}, s32[]{:T(128)}, /*index=5*/s32[]{}, s32...) while((s32[]{:T(128)}, f32[20,10,1326]{2,1,0:T(8,128)S(1)}, ...), condition=%wide.region_4.5_spmd.clone, body=%wide.region_3.4_spmd.sunk.clone.sunk | while | flops 54545016 | bytes 531629 | solution.py:58
  56.4 3.1 fusion.45
  63.7 3.1 fusion.45
  70.9 3.1 fusion.45
  78.2 3.1 fusion.45
  85.5 3.1 fusion.45
  92.7 3.1 fusion.45
  100.0 3.1 fusion.45
  107.3 3.1 fusion.45
  114.5 3.1 fusion.45
  121.8 3.1 fusion.45
  129.1 3.1 fusion.45
  136.3 3.1 fusion.45
  143.6 3.1 fusion.45
  158.1 3.1 fusion.45
  187.2 3.1 fusion.45
  194.4 3.1 fusion.45
  198.8 12.5 %collective-permute-start.1 = (f32[12,10,1326]{2,0,1:T(8,128)S(1)}, f32[12,10,1326]{2,0,1:T(8,128)S(1)}, u32[]{:S(2)}, u32[]{:S(2)}) collective-permute-start(f32[12,10,1326]{2,0,1:T(8,128)S(1)} %copy.19), channel_id=1, source_target_pairs={{0,256},{256,0},{8,264},{264,8},{16,272},{272,16},{24,280},{280,24... | collective-permute-start | bytes 1909448 | tf_op jit(solution)/shard_map/ppermute | solution.py:17
  211.4 19.0 %collective-permute-done.1 = f32[12,10,1326]{2,0,1:T(8,128)S(1)} collective-permute-done((f32[12,10,1326]{2,0,1:T(8,128)S(1)}, f32[12,10,1326]{2,0,1:T(8,128)S(1)}, u32[]{:S(2)}, u32[]{:S(2)}) %collective-permute-start.1) | collective-permute-done | bytes 636512 | tf_op jit(solution)/shard_map/ppermute | solution.py:17
  232.2 21.2 %all-reduce.1 = (f32[5,1326]{1,0:T(8,128)S(1)}, f32[1326]{0:T(1024)S(1)}) all-reduce(f32[5,1326]{1,0:T(8,128)S(1)} %broadcast_multiply_fusion.1, f32[1326]{0:T(1024)S(1)} %broadcast_multiply_fusion.2), channel_id=1, replica_groups=mesh['flop'=64,'turn'=8] {'turn'}, use_global_device_ids=true, to_apply=%region_7.8 | all-reduce | flops 7956 | bytes 63648 | tf_op jit(solution)/shard_map/psum | solution.py:134
  255.3 348.9 %all-reduce = (f32[1,1326]{1,0:T(1,128)S(1)}, f32[1,1326]{1,0:T(1,128)S(1)}) all-reduce(f32[1,1326]{1,0:T(1,128)S(1)} %stack.10, f32[1,1326]{1,0:T(1,128)S(1)} %stack.9), channel_id=1, replica_groups=mesh['flop'=64,'turn'=8] {'flop'}, use_global_device_ids=true, to_apply=%region_14.15 | all-reduce | flops 2652 | bytes 21216 | tf_op jit(solution)/shard_map/psum | solution.py:137
  (177 shorter events, 116.8 us)
Async XLA Ops:
  0.6 10.1 %copy-start.4 = (s32[1326]{0:T(1024)S(1)}, s32[1326]{0:T(1024)}, u32[]{:S(2)}) copy-start(s32[1326]{0:T(1024)} %constant.101.clone) | copy-start | bytes 15916
  0.6 10.1 %copy-start.5 = (s32[1326]{0:T(1024)S(1)}, s32[1326]{0:T(1024)}, u32[]{:S(2)}) copy-start(s32[1326]{0:T(1024)} %constant.102.clone) | copy-start | bytes 15916
  0.7 9.9 %copy-start.3 = (f32[1,5,1326]{2,0,1:T(1,128)S(1)}, f32[1,5,1326]{2,0,1:T(1,128)}, u32[]{:S(2)}) copy-start(f32[1,5,1326]{2,0,1:T(1,128)} %param.15) | copy-start | bytes 79564
  0.7 9.9 %copy-start.8 = (s32[1,4,8]{2,1,0:T(4,128)S(1)}, s32[1,4,8]{2,1,0:T(4,128)}, u32[]{:S(2)}) copy-start(s32[1,4,8]{2,1,0:T(4,128)} %param.19) | copy-start | bytes 388
  0.7 10.1 %copy-start.6 = (s32[1,4,8,1326]{3,2,1,0:T(8,128)S(1)}, s32[1,4,8,1326]{3,2,1,0:T(8,128)}, u32[]{:S(2)}) copy-start(s32[1,4,8,1326]{3,2,1,0:T(8,128)} %param.20) | copy-start | bytes 509188
  12.2 1.4 copy-start.2
  13.6 32.8 %collective-permute-start = (bf16[12,12,1326]{2,1,0:T(8,128)(2,1)}, bf16[12,12,1326]{2,1,0:T(8,128)(2,1)}, u32[]{:S(2)}, u32[]{:S(2)}) collective-permute-start(bf16[12,12,1326]{2,1,0:T(8,128)(2,1)} %pad_maximum_fusion.5), channel_id=1, source_target_pairs={{0,256},{256,0},{8,264},{264,8},{16,272},{272,16},{24,280},{280,24... | collective-permute-start | bytes 1145672 | tf_op jit(solution)/shard_map/ppermute | solution.py:17
  49.1 3.2 copy-start.9
  49.1 3.2 copy-start.10
  49.1 3.2 copy-start.11
  49.1 3.2 copy-start.12
  198.8 31.6 %collective-permute-start.1 = (f32[12,10,1326]{2,0,1:T(8,128)S(1)}, f32[12,10,1326]{2,0,1:T(8,128)S(1)}, u32[]{:S(2)}, u32[]{:S(2)}) collective-permute-start(f32[12,10,1326]{2,0,1:T(8,128)S(1)} %copy.19), channel_id=1, source_target_pairs={{0,256},{256,0},{8,264},{264,8},{16,272},{272,16},{24,280},{280,24... | collective-permute-start | bytes 1909448 | tf_op jit(solution)/shard_map/ppermute | solution.py:17
  230.8 1.1 copy-start.1
  230.8 1.0 copy-start.7
  231.2 22.3 %copy-start = (f32[1,5,4,5,1326]{4,2,3,1,0:T(4,128)S(1)}, f32[1,5,4,5,1326]{4,2,3,1,0:T(4,128)}, u32[]{:S(2)}) copy-start(f32[1,5,4,5,1326]{4,2,3,1,0:T(4,128)} %param.16) | copy-start | bytes 1591204
where the time goes:
time: 609 us; the launch traced here: 605 us
  blocking collectives  370 us (61%)
  matrix products  123 us (20%)
  other arithmetic  37.1 us (6%)
  waiting for transfers between devices  35.3 us (6%)
  starting transfers between devices  28.2 us (5%)
  local copies, waits for them, and re-layouts  9.2 us (2%)
    psum x1, blocking collectives, per_device(): root_zero, root_one = lax.psum((zero_flop, one_flop), 'flop')  349 us
    dot_general x40, matrix products, board_sums(): lax.dot_general(columns, table, (((1,), (1,)), ((), ())), preferred_eleme...  123 us
    ppermute x2, waiting for transfers between devices, swapped(): return lax.ppermute(block, axis, route)  35.3 us
    ppermute x2, starting transfers between devices, swapped(): return lax.ppermute(block, axis, route)  28.2 us
    psum x1, blocking collectives, per_device(): zero_action, one_flop = lax.psum((zero_share, one_share), 'turn')  21.2 us
    add x20, other arithmetic, board_sums(): board_item[width].astype(jnp.float32) * digit_base  16.9 us
  transfers between devices with their start and end apart: 2, of which 2 were waited for; matrix products, arithmetic and copies ran while one was open for 0% of the time, Pallas kernels for 0%

commit v1 on v0

v1 whole, which is shorter than its diff:
```python
import jax
import jax.numpy as jnp
import numpy as np
from jax import lax
from jax.experimental import pallas as pl
from jax.experimental.pallas import tpu as pltpu
from jax.sharding import PartitionSpec as P

HANDS = 1326
ROWS = 1328
WIDTH = 1408
CHUNK = 256
UNROLL = 4
TURNS_ALL = 32


def hand_tables():
    low, high = np.triu_indices(52, 1)
    cards = np.full((2, WIDTH), 99, np.int32)
    cards[0, :HANDS] = low
    cards[1, :HANDS] = high
    share = (low[:, None] == low[None, :]) | (low[:, None] == high[None, :])
    share |= (high[:, None] == low[None, :]) | (high[:, None] == high[None, :])
    apart = np.zeros((ROWS, WIDTH), np.float32)
    apart[:HANDS, :HANDS] = ~share
    return cards, apart


def avoid(low, high, card):
    return jnp.where((low != card) & (high != card), 1.0, 0.0)


def iteration_kernel(
    flop_cards_hbm,
    turn_cards_hbm,
    river_cards_hbm,
    board_count_hbm,
    stakes_hbm,
    reach_hbm,
    flop_reg_hbm,
    turn_reg_hbm,
    ranks_hbm,
    cards_hbm,
    apart_hbm,
    mean_out,
    share,
    flop_cards,
    turn_cards,
    river_cards,
    board_count,
    stakes,
    reach,
    flop_reg,
    turn_reg,
    ranks,
    cards,
    apart,
    columns,
    keys,
    keys_t,
    worth,
    sums,
    arrived,
):
    actions = flop_reg.shape[0]
    turns = turn_reg.shape[2]
    boards = ranks.shape[0]
    rivers = boards // turns
    pairs = (
        (ranks_hbm, ranks),
        (cards_hbm, cards),
        (flop_cards_hbm, flop_cards),
        (turn_cards_hbm, turn_cards),
        (river_cards_hbm, river_cards),
        (board_count_hbm, board_count),
        (stakes_hbm, stakes),
        (reach_hbm, reach),
        (flop_reg_hbm, flop_reg),
        (turn_reg_hbm, turn_reg),
        (apart_hbm, apart),
    )
    copies = [
        pltpu.make_async_copy(source, held, arrived.at[spot])
        for spot, (source, held) in enumerate(pairs)
    ]
    for copy in copies:
        copy.start()

    keys[...] = jnp.zeros(keys.shape, jnp.float32)
    columns[...] = jnp.zeros(columns.shape, jnp.float32)
    sums[...] = jnp.zeros(sums.shape, jnp.float32)
    copies[0].wait()
    drawn = ranks[...]
    power = jnp.exp2((drawn >> 7).astype(jnp.float32))
    mantissa = ((drawn & 127) + 128).astype(jnp.float32)
    keys[:boards, :HANDS] = power * mantissa
    for part in range(WIDTH // 128):
        lanes = slice(part * 128, (part + 1) * 128)
        keys_t[lanes, :] = keys[:, lanes].T
    for copy in copies[1:10]:
        copy.wait()

    low = cards[0:1, :]
    high = cards[1:2, :]
    low_h = cards[0:1, :HANDS]
    high_h = cards[1:2, :HANDS]
    flop_mask = (
        avoid(low_h, high_h, flop_cards[0, 0])
        * avoid(low_h, high_h, flop_cards[0, 1])
        * avoid(low_h, high_h, flop_cards[0, 2])
    )
    turn_mask = jnp.concatenate(
        [avoid(low_h, high_h, turn_cards[0, t]) for t in range(turns)], axis=0
    )
    total = flop_reg[0]
    for a in range(1, actions):
        total = total + flop_reg[a]
    reach_zero = reach[0:1, :] * flop_mask
    for a in range(actions):
        column = reach_zero * (flop_reg[a] / total)
        for t in range(turns):
            columns[t, a : a + 1, :HANDS] = column * turn_mask[t : t + 1, :]
    base = (reach[1:2, :] * flop_mask) * turn_mask
    for a in range(actions):
        total = turn_reg[a, 0]
        for b in range(1, actions):
            total = total + turn_reg[a, b]
        mix = None
        gain = None
        for b in range(actions):
            chance = turn_reg[a, b] / total
            term = stakes[a, b] * (base * chance)
            mix = term if mix is None else mix + term
            term = stakes[a, b] * chance
            gain = term if gain is None else gain + term
        worth[a] = gain
        for t in range(turns):
            columns[t, actions + a : actions + a + 1, :HANDS] = mix[t : t + 1, :]
    copies[10].wait()
    live_count = board_count[0, 0]

    def some_boards(step, carry):
        first = step * UNROLL
        t = first // rivers
        gathered = None
        for ahead in range(UNROLL):
            board = first + ahead
            river_mask = avoid(low, high, river_cards[t, board % rivers])
            mixed = (columns[t] * river_mask).astype(jnp.bfloat16)
            row = keys[pl.ds(board, 1), :].astype(jnp.bfloat16)
            out = None
            for start in range(0, ROWS, CHUNK):
                size = min(CHUNK, ROWS - start)
                rows = slice(start, start + size)
                picked = jnp.full((size, 128), board, jnp.int32)
                column = jnp.take_along_axis(keys_t[rows, :], picked, axis=1)
                column = column.astype(jnp.bfloat16)
                column = jnp.concatenate([column] * (WIDTH // 128), axis=1)
                table = jnp.clip(row - column, -1.0, 1.0) * apart[rows, :]
                part = jnp.dot(mixed[:, rows], table, preferred_element_type=jnp.float32)
                out = part if out is None else out + part
            live = jnp.where(board < live_count, 1.0, 0.0)
            out = out * (river_mask * live)
            gathered = out if gathered is None else gathered + out
        sums[t] = sums[t] + gathered
        return carry

    lax.fori_loop(0, (live_count + (UNROLL - 1)) // UNROLL, some_boards, 0)

    turns_all = TURNS_ALL * 1.0
    zero = None
    for t in range(turns):
        term = sums[t, actions : 2 * actions, :HANDS] * (
            flop_mask * turn_mask[t : t + 1, :]
        )
        zero = term if zero is None else zero + term
    share[0:actions, :] = zero / (rivers * turns_all)
    one_share = None
    for a in range(actions):
        mean = jnp.concatenate([sums[t, a : a + 1, :HANDS] for t in range(turns)], axis=0)
        mean = mean * (flop_mask * turn_mask) / rivers
        mean_out[a] = mean
        node = worth[a] * mean
        one_share = node if one_share is None else one_share + node
    share[actions : actions + 1, :] = jnp.sum(one_share, axis=0, keepdims=True) / turns_all


def iterate(flop_cards, turn_cards, river_cards, board_count, stakes, reach, flop_reg, turn_reg, ranks):
    actions, _, hands = flop_reg.shape
    turns = turn_reg.shape[2]
    cards, apart = hand_tables()
    vmem = pl.BlockSpec(memory_space=pltpu.VMEM)
    operands = (
        flop_cards,
        turn_cards,
        river_cards,
        board_count,
        stakes,
        reach,
        flop_reg,
        turn_reg,
        ranks,
        jnp.asarray(cards),
        jnp.asarray(apart.astype(jnp.bfloat16)),
    )
    return pl.pallas_call(
        iteration_kernel,
        out_shape=(
            jax.ShapeDtypeStruct((actions, turns, hands), jnp.float32),
            jax.ShapeDtypeStruct((actions + 1, hands), jnp.float32),
        ),
        in_specs=[pl.BlockSpec(memory_space=pltpu.HBM)] * len(operands),
        out_specs=(vmem, vmem),
        scratch_shapes=[pltpu.SMEM(held.shape, held.dtype) for held in operands[:5]]
        + [pltpu.VMEM(held.shape, held.dtype) for held in operands[5:]]
        + [
            pltpu.VMEM((turns, 16, WIDTH), jnp.float32),
            pltpu.VMEM((128, WIDTH), jnp.float32),
            pltpu.VMEM((WIDTH, 128), jnp.float32),
            pltpu.VMEM((actions, turns, hands), jnp.float32),
            pltpu.VMEM((turns, 16, WIDTH), jnp.float32),
            pltpu.SemaphoreType.DMA((len(operands),)),
        ],
        compiler_params=pltpu.CompilerParams(vmem_limit_bytes=62 * 1024 * 1024),
        cost_estimate=pl.CostEstimate(
            flops=32 * 2 * 16 * HANDS * HANDS, bytes_accessed=5000000, transcendentals=0
        ),
        name="iteration",
    )(*operands)


def regret_kernel(stakes, mean, turn_reg, turn_next):
    actions = turn_reg.shape[0]
    for a in range(actions):
        total = turn_reg[a, 0]
        for b in range(1, actions):
            total = total + turn_reg[a, b]
        values = [stakes[a, b] * mean[a] for b in range(actions)]
        node = None
        for b in range(actions):
            term = (turn_reg[a, b] / total) * values[b]
            node = term if node is None else node + term
        for b in range(actions):
            turn_next[a, b] = jnp.maximum(turn_reg[a, b] + values[b] - node, 0.0)


def updated(stakes, mean, turn_reg):
    vmem = pl.BlockSpec(memory_space=pltpu.VMEM)
    return pl.pallas_call(
        regret_kernel,
        out_shape=jax.ShapeDtypeStruct(turn_reg.shape, jnp.float32),
        in_specs=[pl.BlockSpec(memory_space=pltpu.SMEM), vmem, vmem],
        out_specs=vmem,
        cost_estimate=pl.CostEstimate(flops=2000000, bytes_accessed=1200000, transcendentals=0),
        name="turn_regrets",
    )(stakes, mean, turn_reg)


def summed(block, axis, groups=None):
    count = lax.axis_size(axis) if groups is None else len(groups[0])
    spread = jnp.broadcast_to(block[None], (count,) + block.shape)
    heard = lax.all_to_all(spread, axis, 0, 0, axis_index_groups=groups, tiled=True)
    return jnp.sum(heard, axis=0)


def tiled(rows):
    count = rows.size
    padded = -(-count // 1024) * 1024
    return jnp.pad(rows.reshape(-1), (0, padded - count)).reshape(-1, 128)


def per_device(
    root_reach,
    stakes,
    flop_regrets,
    turn_regrets,
    flop_cards,
    turn_cards,
    river_cards,
    hand_ranks,
    board_count,
):
    actions = flop_regrets.shape[1]
    hands = flop_regrets.shape[2]
    turns = turn_cards.shape[1]
    rivers = river_cards.shape[2]
    flop_reg = jnp.transpose(flop_regrets, (1, 0, 2))
    turn_reg = jnp.transpose(turn_regrets[0], (0, 2, 1, 3))
    mean, share = iterate(
        flop_cards,
        turn_cards,
        river_cards[0],
        board_count,
        stakes,
        root_reach,
        flop_reg,
        turn_reg,
        hand_ranks.reshape(turns * rivers, hands),
    )
    turn_new = updated(stakes, mean, turn_reg)
    total = summed(tiled(share), "turn").reshape(-1)[: share.size].reshape(share.shape)
    regrets = flop_regrets[0]
    flop_policy = regrets / jnp.sum(regrets, axis=0, keepdims=True)
    zero_action = total[:actions]
    zero_flop = jnp.sum(flop_policy * zero_action, axis=0)
    flop_next = jnp.maximum(regrets + zero_action - zero_flop, 0.0)[None]
    values = tiled(jnp.stack([zero_flop, total[actions]]))
    values, flop_next, turn_new = lax.optimization_barrier((values, flop_next, turn_new))
    turn_next = jnp.transpose(turn_new, (0, 2, 1, 3))[None]
    flops = lax.axis_size("flop")
    near = [list(range(i, i + 4)) for i in range(0, flops, 4)]
    far = [list(range(i, flops, 4)) for i in range(4)]
    values = summed(summed(values, "flop", near), "flop", far)
    root_values = values.reshape(-1)[: 2 * hands].reshape(2, hands)
    return (flop_next, turn_next, root_values)


def solution(mesh):
    in_specs = (
        P(),
        P(),
        P("flop", None, None),
        P("flop", None, "turn", None, None),
        P("flop", None),
        P("flop", "turn"),
        P("flop", "turn", None),
        P("flop", "turn", None, None),
        P("flop", "turn"),
    )
    out_specs = (P("flop", None, None), P("flop", None, "turn", None, None), P())
    return jax.shard_map(
        per_device, mesh=mesh, in_specs=in_specs, out_specs=out_specs, check_vma=False
    )
```

time: 609 us -> 76 us (0.12)
  the two profiles are of different devices: /device:TPU:2 before, /device:TPU:32 now
where the time goes in v1:
time: 76 us; the launch traced here: 75.6 us
  blocking collectives  40.4 us (53%)
  Pallas kernels  20.7 us (27%)
  waiting for transfers between devices  5.39 us (7%)
  starting transfers between devices  4.3 us (6%)
  local copies, waits for them, and re-layouts  2.65 us (3%)
  between operations  1.37 us (2%)
  other arithmetic  0.77 us (1%)
    all_to_all x2, blocking collectives, summed(): lax.all_to_all(spread, axis, 0, 0, axis_index_groups=groups, tiled=True)  40.4 us
    pallas_call x1, Pallas kernels, iterate(): pl.pallas_call(iteration_kernel, out_shape=(jax.ShapeDtypeStruct((actions...  18.6 us
    all_to_all x1, waiting for transfers between devices, summed(): lax.all_to_all(spread, axis, 0, 0, axis_index_groups=groups, tiled=True)  5.39 us
    all_to_all x1, starting transfers between devices, summed(): lax.all_to_all(spread, axis, 0, 0, axis_index_groups=groups, tiled=True)  4.3 us
    pallas_call x1, Pallas kernels, updated(): pl.pallas_call(regret_kernel, out_shape=jax.ShapeDtypeStruct(turn_reg.sha...  2.1 us
  transfers between devices with their start and end apart: 1, of which 1 were waited for; matrix products, arithmetic and copies ran while one was open for 0% of the time, Pallas kernels for 3%

profile of v1, /device:TPU:32, one launch (start us, length us, event | category | flops | bytes accessed | tf_op | source)
XLA Modules:
  0.0 75.6 jit_solution(17503371660807635726)
XLA Ops:
  1.3 0.0 copy-start
  1.3 18.6 %iteration.1 = (f32[5,4,1326]{2,1,0:T(4,128)}, f32[6,1326]{1,0:T(8,128)}) custom-call(s32[1,3]{1,0:T(1,128)} %flop_cards_hbm.1, s32[1,4]{1,0:T(1,128)} %turn_cards_hbm.1, s32[4,8]{1,0:T(4,128)} %bitcast.30, s32[1,1]{1,0:T(1,128)S(6)} %copy.18.board_count_hbm, f32[5,5]{1,0:T(8,128)} %stakes.1, f32[2,1326]{1,0:T(2,128)} %reach_hbm.1, f32[5,1,1326]{2,1,0:T(1,128)} %bitcast.25, ...), custom_call_target="tpu_custom_call" | custom-call | flops 1800474624 | bytes 5000000 | tf_op jit(solution)/shard_map/iteration/pallas_call | solution.py:206
  19.9 0.9 %reshape.43 = f32[7956]{0:T(1024)S(1)} reshape(f32[6,1326]{1,0:T(8,128)} %get-tuple-element.8) | data formatting | bytes 63648 | tf_op jit(solution)/shard_map/reshape | solution.py:269
  20.8 0.7 broadcast_in_dim.11
  21.5 4.3 %all-to-all-start = ((f32[8,64,128]{2,1,0:T(8,128)}), f32[8,64,128]{2,1,0:T(8,128)S(1)}, u32[]{:S(2)}, u32[]{:S(2)}) async-start(f32[8,64,128]{2,1,0:T(8,128)} %broadcast_in_dim.11), calls=%async_computation | async-start | bytes 524288 | tf_op jit(solution)/shard_map/all_to_all | solution.py:262
  25.8 0.0 copy-done
  25.9 2.1 %turn_regrets.1 = f32[5,5,4,1326]{3,2,1,0:T(4,128)} custom-call(f32[5,5]{1,0:T(8,128)} %stakes.1, f32[5,4,1326]{2,1,0:T(4,128)} %get-tuple-element.9.mean, f32[5,5,4,1326]{3,2,1,0:T(4,128)} %bitcast.23), custom_call_target="tpu_custom_call" | custom-call | flops 2000000 | bytes 1200000 | tf_op jit(solution)/shard_map/turn_regrets/pallas_call | solution.py:249
  28.0 5.4 %all-to-all-done = f32[8,64,128]{2,1,0:T(8,128)S(1)} async-done(((f32[8,64,128]{2,1,0:T(8,128)}), f32[8,64,128]{2,1,0:T(8,128)S(1)}, u32[]{:S(2)}, u32[]{:S(2)}) %all-to-all-start) | async-done | bytes 262176 | tf_op jit(solution)/shard_map/all_to_all | solution.py:262
  33.4 0.1 slice.27
  33.5 0.1 slice.24
  33.6 0.1 slice.21
  33.7 0.7 subtract_maximum_fusion
  34.4 0.1 reshape.45
  34.5 9.9 %all_to_all.15 = f32[4,24,128]{2,1,0:T(8,128)S(1)} all-to-all(f32[4,24,128]{2,1,0:T(8,128)S(1)} %broadcast_in_dim.13), channel_id=1, replica_groups={{0,8,16,24},{32,40,48,56},{64,72,80,88},{96,104,112,120},{128,136,144,1..., dimensions={0} | all-to-all | bytes 98304 | tf_op jit(solution)/shard_map/all_to_all | solution.py:262
  44.4 30.5 %all_to_all.16 = f32[16,24,128]{2,1,0:T(8,128)S(1)} all-to-all(f32[16,24,128]{2,1,0:T(8,128)S(1)} %broadcast_in_dim.14), channel_id=1, replica_groups={{0,32,64,96,128,160,192,224,256,288,320,352,384,416,448,480},{8,40,72,1..., dimensions={0} | all-to-all | bytes 393216 | tf_op jit(solution)/shard_map/all_to_all | solution.py:262
  74.9 0.7 reshape.48
  (13 shorter events, 0.2 us)
Async XLA Ops:
  1.3 24.5 %copy-start = (f32[1,5,1326]{2,0,1:T(1,128)S(1)}, f32[1,5,1326]{2,0,1:T(1,128)}, u32[]{:S(2)}) copy-start(f32[1,5,1326]{2,0,1:T(1,128)} %param.13) | copy-start | bytes 79564
  21.5 11.8 %all-to-all-start = ((f32[8,64,128]{2,1,0:T(8,128)}), f32[8,64,128]{2,1,0:T(8,128)S(1)}, u32[]{:S(2)}, u32[]{:S(2)}) async-start(f32[8,64,128]{2,1,0:T(8,128)} %broadcast_in_dim.11), calls=%async_computation | async-start | bytes 524288 | tf_op jit(solution)/shard_map/all_to_all | solution.py:262

commit v2 on v1

v2 whole, which is shorter than its diff:
```python
import jax
import jax.numpy as jnp
import numpy as np
from jax import lax
from jax.experimental import pallas as pl
from jax.experimental.pallas import tpu as pltpu
from jax.sharding import PartitionSpec as P

HANDS = 1326
WIDTH = 1408
DECK = 48
LIVE = 1128
ROWS = 1136
SPAN = 1152
SHIFTS = 8
CHUNK = 256
UNROLL = 8
TURNS_ALL = 32
DEVICES = 8
LINES = 72


def hand_tables():
    low, high = np.triu_indices(52, 1)
    cards = np.full((2, WIDTH), 99, np.int32)
    cards[0, :HANDS] = low
    cards[1, :HANDS] = high
    low, high = np.triu_indices(DECK, 1)
    share = (low[:, None] == low[None, :]) | (low[:, None] == high[None, :])
    share |= (high[:, None] == low[None, :]) | (high[:, None] == high[None, :])
    apart = np.zeros((ROWS, SPAN), np.float32)
    apart[:LIVE, :LIVE] = ~share
    return cards, apart


def avoid(low, high, card):
    return jnp.where((low != card) & (high != card), 1.0, 0.0)


def below(card, cards):
    count = (card > cards[0]).astype(jnp.int32)
    for other in cards[1:]:
        count = count + (card > other).astype(jnp.int32)
    return count


def iteration_kernel(
    flop_cards_hbm,
    turn_cards_hbm,
    river_cards_hbm,
    board_count_hbm,
    stakes_hbm,
    cards_hbm,
    ranks_hbm,
    reach_hbm,
    flop_reg_hbm,
    turn_reg_hbm,
    apart_hbm,
    mean_out,
    message,
    flop_cards,
    turn_cards,
    river_cards,
    board_count,
    stakes,
    cards,
    ranks,
    reach,
    flop_reg,
    turn_reg,
    apart,
    wide,
    moves,
    arrivals,
    keys,
    keys_t,
    columns,
    worth,
    sums,
    others,
    lines,
    arrived,
):
    actions = flop_reg.shape[0]
    turns = turn_reg.shape[2]
    boards = ranks.shape[0]
    rivers = boards // turns
    pairs = (
        (flop_cards_hbm, flop_cards),
        (turn_cards_hbm, turn_cards),
        (river_cards_hbm, river_cards),
        (board_count_hbm, board_count),
        (stakes_hbm, stakes),
        (cards_hbm, cards),
        (ranks_hbm, ranks),
        (reach_hbm, reach),
        (flop_reg_hbm, flop_reg),
        (turn_reg_hbm, turn_reg),
        (apart_hbm, apart),
    )
    copies = [
        pltpu.make_async_copy(source, held, arrived.at[spot])
        for spot, (source, held) in enumerate(pairs)
    ]
    for copy in copies:
        copy.start()

    tail = slice(WIDTH - 128, WIDTH)
    wide[:, :, tail] = jnp.zeros((turns + 1, 16, 128), jnp.float32)
    sums[...] = jnp.zeros(sums.shape, jnp.float32)
    lines[...] = jnp.zeros(lines.shape, jnp.float32)
    for t in range(turns):
        columns[t, 8:16, :] = jnp.zeros((8, SPAN), jnp.float32)
    for copy in copies[:6]:
        copy.wait()

    shape = (2 * turns, WIDTH)
    low = jnp.broadcast_to(cards[0:1, :], shape)
    high = jnp.broadcast_to(cards[1:2, :], shape)
    place = lax.broadcasted_iota(jnp.int32, shape, 1)
    which = lax.broadcasted_iota(jnp.int32, shape, 0) >> 1
    turn_card = jnp.full(shape, turn_cards[0, 0], jnp.int32)
    for t in range(1, turns):
        turn_card = jnp.where(which == t, turn_cards[0, t], turn_card)
    gone = [flop_cards[0, 0], flop_cards[0, 1], flop_cards[0, 2], turn_card]
    mask = (low != gone[0]) & (high != gone[0])
    for card in gone[1:]:
        mask = mask & (low != card) & (high != card)
    first = low - below(low, gone)
    second = high - below(high, gone)
    index = ((first * (2 * DECK - 1 - first)) >> 1) + second - first - 1
    chosen = jnp.where(mask, 1.0, 0.0)
    weight = jnp.concatenate([chosen[2 * t : 2 * t + 1, :HANDS] for t in range(turns)], axis=0)
    lag = jnp.where(mask & (place < HANDS), place - index, 0)
    for shift in range(SHIFTS):
        step = 1 << shift
        move = (lag >> shift) & 1
        came = pltpu.roll(move, WIDTH - step, 1)
        moves[shift] = move
        arrivals[shift] = came.astype(jnp.float32)
        lag = jnp.where(
            came == 1, pltpu.roll(lag, WIDTH - step, 1), jnp.where(move == 1, 0, lag)
        )

    copies[6].wait()
    drawn = ranks[...]
    power = jnp.exp2((drawn >> 7).astype(jnp.float32))
    mantissa = ((drawn & 127) + 128).astype(jnp.float32)
    drawn = power * mantissa
    for t in range(turns):
        wide[t, 0:rivers, :HANDS] = drawn[t * rivers : (t + 1) * rivers, :]
    both = cards[...].astype(jnp.float32)
    for t in range(turns):
        wide[turns, 8 + 2 * t : 10 + 2 * t, :] = both
    for copy in copies[7:10]:
        copy.wait()
    total = flop_reg[0]
    for a in range(1, actions):
        total = total + flop_reg[a]
    for a in range(actions):
        column = reach[0:1, :] * (flop_reg[a] / total)
        for t in range(turns):
            wide[t, 8 + a : 9 + a, :HANDS] = column
    base = reach[1:2, :]
    for a in range(actions):
        total = turn_reg[a, 0]
        for b in range(1, actions):
            total = total + turn_reg[a, b]
        mix = None
        gain = None
        for b in range(actions):
            chance = turn_reg[a, b] / total
            term = stakes[a, b] * (base * chance)
            mix = term if mix is None else mix + term
            term = stakes[a, b] * chance
            gain = term if gain is None else gain + term
        worth[a] = gain
        for t in range(turns):
            if a < 3:
                wide[t, 13 + a : 14 + a, :HANDS] = mix[t : t + 1, :]
            else:
                spot = 2 * t + a - 3
                wide[turns, spot : spot + 1, :HANDS] = mix[t : t + 1, :]

    for t in range(turns + 1):
        rows = wide[t].astype(jnp.bfloat16)
        for shift in range(SHIFTS):
            step = 1 << shift
            if t < turns:
                came = arrivals[shift, 2 * t : 2 * t + 1, :].astype(jnp.bfloat16)
                came = jnp.broadcast_to(came, rows.shape)
            else:
                came = arrivals[shift]
                came = jnp.concatenate([came, came], axis=0).astype(jnp.bfloat16)
            rows = jnp.where(came > 0.5, pltpu.roll(rows, WIDTH - step, 1), rows)
        rows = rows.astype(jnp.float32)
        if t < turns:
            keys[t * rivers : (t + 1) * rivers, :] = rows[0:8, :SPAN]
            columns[t, 0:8, :] = rows[8:16, :SPAN]
        else:
            for other in range(turns):
                columns[other, 8:10, :] = rows[2 * other : 2 * other + 2, :SPAN]
                columns[other, 10:12, :] = rows[8 + 2 * other : 10 + 2 * other, :SPAN]
    for part in range(SPAN // 128):
        lanes = slice(part * 128, (part + 1) * 128)
        keys_t[lanes, 0:boards] = keys[:, lanes].T
    copies[10].wait()
    live_count = board_count[0, 0]

    def some_boards(step, carry):
        origin = step * UNROLL
        t = origin // rivers
        held = columns[t]
        low_live = held[10:11, :].astype(jnp.int32)
        high_live = held[11:12, :].astype(jnp.int32)
        gathered = None
        for ahead in range(UNROLL):
            board = origin + ahead
            river_mask = avoid(low_live, high_live, river_cards[t, board % rivers])
            mixed = (held * river_mask).astype(jnp.bfloat16)
            row = keys[pl.ds(board, 1), :].astype(jnp.bfloat16)
            out = None
            for start in range(0, ROWS, CHUNK):
                size = min(CHUNK, ROWS - start)
                rows = slice(start, start + size)
                picked = jnp.full((size, 128), board, jnp.int32)
                column = jnp.take_along_axis(keys_t[rows, :], picked, axis=1)
                column = column.astype(jnp.bfloat16)
                column = jnp.concatenate([column] * (SPAN // 128), axis=1)
                table = jnp.clip(row - column, -1.0, 1.0) * apart[rows, :]
                part = jnp.dot(mixed[:, rows], table, preferred_element_type=jnp.float32)
                out = part if out is None else out + part
            live = jnp.where(board < live_count, 1.0, 0.0)
            out = out * (river_mask * live)
            gathered = out if gathered is None else gathered + out
        sums[t, :, :SPAN] = sums[t, :, :SPAN] + gathered
        return carry

    lax.fori_loop(0, (live_count + (UNROLL - 1)) // UNROLL, some_boards, 0)

    for t in range(turns):
        others[2 * t : 2 * t + 2, :] = sums[t, 8:10, :]
    for t in range(turns + 1):
        rows = sums[t, 0:8, :] if t < turns else others[...]
        for shift in reversed(range(SHIFTS)):
            step = 1 << shift
            move = moves[shift, 2 * t : 2 * t + 1, :] if t < turns else moves[shift]
            move = jnp.broadcast_to(move, rows.shape)
            rows = jnp.where(move == 1, pltpu.roll(rows, step, 1), rows)
        if t < turns:
            sums[t, 0:8, :] = rows
        else:
            others[...] = rows
    zero = None
    for t in range(turns):
        term = jnp.concatenate(
            [sums[t, actions:8, :HANDS], others[2 * t : 2 * t + 2, :HANDS]], axis=0
        )
        term = term * weight[t : t + 1, :]
        zero = term if zero is None else zero + term
    zero = zero / (rivers * TURNS_ALL * 1.0)
    one_share = None
    for a in range(actions):
        mean = jnp.concatenate([sums[t, a : a + 1, :HANDS] for t in range(turns)], axis=0)
        mean = mean * weight / rivers
        mean_out[a] = mean
        node = worth[a] * mean
        one_share = node if one_share is None else one_share + node
    one_share = jnp.sum(one_share, axis=0, keepdims=True) / (TURNS_ALL * 1.0)
    tiles = WIDTH // 128
    for a in range(actions + 1):
        row = zero[a : a + 1, :] if a < actions else one_share
        for part in range(tiles):
            ends = min((part + 1) * 128, HANDS)
            line = a * tiles + part
            lines[line : line + 1, 0 : ends - part * 128] = row[:, part * 128 : ends]
    for device in range(message.shape[0]):
        message[device] = lines[...]


def iterate(flop_cards, turn_cards, river_cards, board_count, stakes, reach, flop_reg, turn_reg, ranks):
    actions, _, hands = flop_reg.shape
    turns = turn_reg.shape[2]
    boards = ranks.shape[0]
    cards, apart = hand_tables()
    vmem = pl.BlockSpec(memory_space=pltpu.VMEM)
    operands = (
        flop_cards,
        turn_cards,
        river_cards,
        board_count,
        stakes,
        jnp.asarray(cards),
        ranks,
        reach,
        flop_reg,
        turn_reg,
        jnp.asarray(apart.astype(jnp.bfloat16)),
    )
    return pl.pallas_call(
        iteration_kernel,
        out_shape=(
            jax.ShapeDtypeStruct((actions, turns, hands), jnp.float32),
            jax.ShapeDtypeStruct((DEVICES, LINES, 128), jnp.float32),
        ),
        in_specs=[pl.BlockSpec(memory_space=pltpu.HBM)] * len(operands),
        out_specs=(vmem, vmem),
        scratch_shapes=[pltpu.SMEM(held.shape, held.dtype) for held in operands[:5]]
        + [pltpu.VMEM(held.shape, held.dtype) for held in operands[5:]]
        + [
            pltpu.VMEM((turns + 1, 16, WIDTH), jnp.float32),
            pltpu.VMEM((SHIFTS, 2 * turns, WIDTH), jnp.int32),
            pltpu.VMEM((SHIFTS, 2 * turns, WIDTH), jnp.float32),
            pltpu.VMEM((boards, SPAN), jnp.float32),
            pltpu.VMEM((SPAN, 128), jnp.float32),
            pltpu.VMEM((turns, 16, SPAN), jnp.float32),
            pltpu.VMEM((actions, turns, hands), jnp.float32),
            pltpu.VMEM((turns, 16, WIDTH), jnp.float32),
            pltpu.VMEM((2 * turns, WIDTH), jnp.float32),
            pltpu.VMEM((LINES, 128), jnp.float32),
            pltpu.SemaphoreType.DMA((len(operands),)),
        ],
        compiler_params=pltpu.CompilerParams(vmem_limit_bytes=62 * 1024 * 1024),
        cost_estimate=pl.CostEstimate(
            flops=32 * 2 * 16 * HANDS * HANDS, bytes_accessed=5000000, transcendentals=0
        ),
        name="iteration",
    )(*operands)


def regret_kernel(stakes, mean, turn_reg, turn_next):
    actions = turn_reg.shape[0]
    for a in range(actions):
        total = turn_reg[a, 0]
        for b in range(1, actions):
            total = total + turn_reg[a, b]
        values = [stakes[a, b] * mean[a] for b in range(actions)]
        node = None
        for b in range(actions):
            term = (turn_reg[a, b] / total) * values[b]
            node = term if node is None else node + term
        for b in range(actions):
            turn_next[a, b] = jnp.maximum(turn_reg[a, b] + values[b] - node, 0.0)


def updated(stakes, mean, turn_reg):
    vmem = pl.BlockSpec(memory_space=pltpu.VMEM)
    return pl.pallas_call(
        regret_kernel,
        out_shape=jax.ShapeDtypeStruct(turn_reg.shape, jnp.float32),
        in_specs=[pl.BlockSpec(memory_space=pltpu.SMEM), vmem, vmem],
        out_specs=vmem,
        cost_estimate=pl.CostEstimate(flops=2000000, bytes_accessed=1200000, transcendentals=0),
        name="turn_regrets",
    )(stakes, mean, turn_reg)


def summed(block, axis, groups=None):
    count = lax.axis_size(axis) if groups is None else len(groups[0])
    spread = jnp.broadcast_to(block[None], (count,) + block.shape)
    heard = lax.all_to_all(spread, axis, 0, 0, axis_index_groups=groups, tiled=True)
    return jnp.sum(heard, axis=0)


def tiled(rows):
    count = rows.size
    padded = -(-count // 1024) * 1024
    return jnp.pad(rows.reshape(-1), (0, padded - count)).reshape(-1, 128)


def per_device(
    root_reach,
    stakes,
    flop_regrets,
    turn_regrets,
    flop_cards,
    turn_cards,
    river_cards,
    hand_ranks,
    board_count,
):
    actions = flop_regrets.shape[1]
    hands = flop_regrets.shape[2]
    turns = turn_cards.shape[1]
    rivers = river_cards.shape[2]
    flop_reg = jnp.transpose(flop_regrets, (1, 0, 2))
    turn_reg = jnp.transpose(turn_regrets[0], (0, 2, 1, 3))
    mean, message = iterate(
        flop_cards,
        turn_cards,
        river_cards[0],
        board_count,
        stakes,
        root_reach,
        flop_reg,
        turn_reg,
        hand_ranks.reshape(turns * rivers, hands),
    )
    heard = lax.all_to_all(message, "turn", 0, 0, tiled=True)
    heard = jnp.sum(heard, axis=0)[: (actions + 1) * (WIDTH // 128)]
    total = heard.reshape(actions + 1, WIDTH)[:, :hands]
    regrets = flop_regrets[0]
    flop_policy = regrets / jnp.sum(regrets, axis=0, keepdims=True)
    zero_flop = jnp.sum(flop_policy * total[:actions], axis=0)
    values = tiled(jnp.stack([zero_flop, total[actions]]))
    flops = lax.axis_size("flop")
    near = [list(range(i, i + 4)) for i in range(0, flops, 4)]
    far = [list(range(i, flops, 4)) for i in range(4)]
    values = summed(values, "flop", near)
    values, total, zero_flop, mean = lax.optimization_barrier((values, total, zero_flop, mean))
    turn_new = updated(stakes, mean, turn_reg)
    turn_next = jnp.transpose(turn_new, (0, 2, 1, 3))[None]
    flop_next = jnp.maximum(regrets + total[:actions] - zero_flop, 0.0)[None]
    values = summed(values, "flop", far)
    root_values = values.reshape(-1)[: 2 * hands].reshape(2, hands)
    return (flop_next, turn_next, root_values)


def solution(mesh):
    in_specs = (
        P(),
        P(),
        P("flop", None, None),
        P("flop", None, "turn", None, None),
        P("flop", None),
        P("flop", "turn"),
        P("flop", "turn", None),
        P("flop", "turn", None, None),
        P("flop", "turn"),
    )
    out_specs = (P("flop", None, None), P("flop", None, "turn", None, None), P())
    return jax.shard_map(
        per_device, mesh=mesh, in_specs=in_specs, out_specs=out_specs, check_vma=False
    )
```

time: 76 us -> 70.1 us (0.922)
  blocking collectives: 40.4 us -> 8.85 us
  starting transfers between devices: 4.3 us -> 19.6 us
  waiting for transfers between devices: 5.39 us -> 19.5 us
  Pallas kernels: 20.7 us -> 18.2 us
    all_to_all x2 -> x1, blocking collectives: 40.4 us -> 8.85 us  [summed(): lax.all_to_all(spread, axis, 0, 0, axis_index_groups=groups, tiled=True)]
    all_to_all x1, starting transfers between devices: 4.3 us -> 15.3 us  [summed(): lax.all_to_all(spread, axis, 0, 0, axis_index_groups=groups, tiled=True)]
    all_to_all x0 -> x1, waiting for transfers between devices: none -> 7.85 us  [per_device(): heard = lax.all_to_all(message, 'turn', 0, 0, tiled=True)]
    all_to_all x1, waiting for transfers between devices: 5.39 us -> 11.7 us  [summed(): lax.all_to_all(spread, axis, 0, 0, axis_index_groups=groups, tiled=True)]
    all_to_all x0 -> x1, starting transfers between devices: none -> 4.31 us  [per_device(): heard = lax.all_to_all(message, 'turn', 0, 0, tiled=True)]
    pallas_call x1, Pallas kernels: 18.6 us -> 16.1 us  [iterate(): pl.pallas_call(iteration_kernel, out_shape=(jax.ShapeDtypeStruct((actions...]
    reshape x3 -> x1, local copies, waits for them, and re-layouts: 0.96 us -> 0.08 us  [tiled(): return jnp.pad(rows.reshape(-1), (0, padded - count)).reshape(-1, 128)]
  transfers between devices with their start and end apart: 1 -> 2, of which waited for: 1 -> 2; matrix products, arithmetic and copies ran while one was open for 0% -> 1% of each run, Pallas kernels for 3% -> 3%
where the time goes in v2:
time: 70.1 us; the launch traced here: 69.8 us
  starting transfers between devices  19.6 us (28%)
  waiting for transfers between devices  19.5 us (28%)
  Pallas kernels  18.2 us (26%)
  blocking collectives  8.85 us (13%)
  local copies, waits for them, and re-layouts  2.12 us (3%)
  between operations  1.36 us (2%)
    pallas_call x1, Pallas kernels, iterate(): pl.pallas_call(iteration_kernel, out_shape=(jax.ShapeDtypeStruct((actions...  16.1 us
    all_to_all x1, starting transfers between devices, summed(): lax.all_to_all(spread, axis, 0, 0, axis_index_groups=groups, tiled=True)  15.3 us
    all_to_all x1, waiting for transfers between devices, summed(): lax.all_to_all(spread, axis, 0, 0, axis_index_groups=groups, tiled=True)  11.7 us
    all_to_all x1, blocking collectives, summed(): lax.all_to_all(spread, axis, 0, 0, axis_index_groups=groups, tiled=True)  8.85 us
    all_to_all x1, waiting for transfers between devices, per_device(): heard = lax.all_to_all(message, 'turn', 0, 0, tiled=True)  7.85 us
    all_to_all x1, starting transfers between devices, per_device(): heard = lax.all_to_all(message, 'turn', 0, 0, tiled=True)  4.31 us
    pallas_call x1, Pallas kernels, updated(): pl.pallas_call(regret_kernel, out_shape=jax.ShapeDtypeStruct(turn_reg.sha...  2.1 us
  transfers between devices with their start and end apart: 2, of which 2 were waited for; matrix products, arithmetic and copies ran while one was open for 1% of the time, Pallas kernels for 3%

profile of v2, /device:TPU:32, one launch (start us, length us, event | category | flops | bytes accessed | tf_op | source)
XLA Modules:
  0.0 69.8 jit_solution(9789892007337763)
XLA Ops:
  1.3 0.0 copy-start
  1.3 16.1 %iteration.1 = (f32[5,4,1326]{2,1,0:T(4,128)}, f32[8,72,128]{2,1,0:T(8,128)}) custom-call(s32[1,3]{1,0:T(1,128)} %flop_cards_hbm.1, s32[1,4]{1,0:T(1,128)} %turn_cards_hbm.1, s32[4,8]{1,0:T(4,128)} %bitcast.32, s32[1,1]{1,0:T(1,128)S(6)} %copy.23.board_count_hbm, f32[5,5]{1,0:T(8,128)} %stakes.1, s32[2,1408]{1,0:T(2,128)} %constant.4.clone.cards_hbm, ...), custom_call_target="tpu_custom_call" | custom-call | flops 1800474624 | bytes 5000000 | tf_op jit(solution)/shard_map/iteration/pallas_call | solution.py:300
  17.4 4.3 %all-to-all-start = ((f32[8,72,128]{2,1,0:T(8,128)}), f32[8,72,128]{2,1,0:T(8,128)S(1)}, u32[]{:S(2)}, u32[]{:S(2)}) async-start(f32[8,72,128]{2,1,0:T(8,128)} %get-tuple-element.9), calls=%async_computation | async-start | bytes 589824 | tf_op jit(solution)/shard_map/all_to_all | solution.py:399
  21.7 0.0 copy-done
  21.7 7.8 %all-to-all-done = f32[8,72,128]{2,1,0:T(8,128)S(1)} async-done(((f32[8,72,128]{2,1,0:T(8,128)}), f32[8,72,128]{2,1,0:T(8,128)S(1)}, u32[]{:S(2)}, u32[]{:S(2)}) %all-to-all-start) | async-done | bytes 294944 | tf_op jit(solution)/shard_map/all_to_all | solution.py:399
  29.7 0.1 reshape.27
  29.8 8.8 %all_to_all.15 = f32[4,24,128]{2,1,0:T(8,128)S(1)} all-to-all(f32[4,24,128]{2,1,0:T(8,128)S(1)} %broadcast_in_dim.22), channel_id=1, replica_groups={{0,8,16,24},{32,40,48,56},{64,72,80,88},{96,104,112,120},{128,136,144,1..., dimensions={0} | all-to-all | bytes 98304 | tf_op jit(solution)/shard_map/all_to_all | solution.py:361
  38.6 0.7 broadcast_in_dim.25
  39.3 15.3 %all-to-all-start.2 = ((f32[16,24,128]{2,1,0:T(8,128)}), f32[16,24,128]{2,1,0:T(8,128)S(1)}, u32[]{:S(2)}, u32[]{:S(2)}) async-start(f32[16,24,128]{2,1,0:T(8,128)} %broadcast_in_dim.25), calls=%async_computation.2 | async-start | bytes 393216 | tf_op jit(solution)/shard_map/all_to_all | solution.py:361
  54.7 0.6 broadcast_in_dim.23
  55.3 2.1 %turn_regrets.1 = f32[5,5,4,1326]{3,2,1,0:T(4,128)} custom-call(f32[5,5]{1,0:T(8,128)} %stakes.1, f32[5,4,1326]{2,1,0:T(4,128)} %get-tuple-element.13.mean, f32[5,5,4,1326]{3,2,1,0:T(4,128)} %bitcast.25), custom_call_target="tpu_custom_call" | custom-call | flops 2000000 | bytes 1200000 | tf_op jit(solution)/shard_map/turn_regrets/pallas_call | solution.py:348
  57.4 11.7 %all-to-all-done.2 = f32[16,24,128]{2,1,0:T(8,128)S(1)} async-done(((f32[16,24,128]{2,1,0:T(8,128)}), f32[16,24,128]{2,1,0:T(8,128)S(1)}, u32[]{:S(2)}, u32[]{:S(2)}) %all-to-all-start.2) | async-done | bytes 196640 | tf_op jit(solution)/shard_map/all_to_all | solution.py:361
  69.1 0.7 reshape.29
  (12 shorter events, 0.2 us)
Async XLA Ops:
  1.3 20.4 %copy-start = (f32[1,5,1326]{2,0,1:T(1,128)S(1)}, f32[1,5,1326]{2,0,1:T(1,128)}, u32[]{:S(2)}) copy-start(f32[1,5,1326]{2,0,1:T(1,128)} %param.13) | copy-start | bytes 79564
  17.4 12.2 %all-to-all-start = ((f32[8,72,128]{2,1,0:T(8,128)}), f32[8,72,128]{2,1,0:T(8,128)S(1)}, u32[]{:S(2)}, u32[]{:S(2)}) async-start(f32[8,72,128]{2,1,0:T(8,128)} %get-tuple-element.9), calls=%async_computation | async-start | bytes 589824 | tf_op jit(solution)/shard_map/all_to_all | solution.py:399
  39.3 29.7 %all-to-all-start.2 = ((f32[16,24,128]{2,1,0:T(8,128)}), f32[16,24,128]{2,1,0:T(8,128)S(1)}, u32[]{:S(2)}, u32[]{:S(2)}) async-start(f32[16,24,128]{2,1,0:T(8,128)} %broadcast_in_dim.25), calls=%async_computation.2 | async-start | bytes 393216 | tf_op jit(solution)/shard_map/all_to_all | solution.py:361

commit v3 on v2

--- a/solution.py
+++ b/solution.py
@@ -14,10 +14,9 @@
 SPAN = 1152
 SHIFTS = 8
 CHUNK = 256
-UNROLL = 8
+UNROLL = 16
 TURNS_ALL = 32
 DEVICES = 8
-LINES = 72
 
 
 def hand_tables():
@@ -78,7 +77,6 @@
     worth,
     sums,
     others,
-    lines,
     arrived,
 ):
     actions = flop_reg.shape[0]
@@ -108,7 +106,6 @@
     tail = slice(WIDTH - 128, WIDTH)
     wide[:, :, tail] = jnp.zeros((turns + 1, 16, 128), jnp.float32)
     sums[...] = jnp.zeros(sums.shape, jnp.float32)
-    lines[...] = jnp.zeros(lines.shape, jnp.float32)
     for t in range(turns):
         columns[t, 8:16, :] = jnp.zeros((8, SPAN), jnp.float32)
     for copy in copies[:6]:
@@ -208,13 +205,14 @@
     live_count = board_count[0, 0]
 
     def some_boards(step, carry):
-        origin = step * UNROLL
-        t = origin // rivers
+      for part in range(UNROLL // rivers):
+        origin = step * UNROLL + part * rivers
+        t = step * (UNROLL // rivers) + part
         held = columns[t]
         low_live = held[10:11, :].astype(jnp.int32)
         high_live = held[11:12, :].astype(jnp.int32)
         gathered = None
-        for ahead in range(UNROLL):
+        for ahead in range(rivers):
             board = origin + ahead
             river_mask = avoid(low_live, high_live, river_cards[t, board % rivers])
             mixed = (held * river_mask).astype(jnp.bfloat16)
@@ -234,7 +232,7 @@
             out = out * (river_mask * live)
             gathered = out if gathered is None else gathered + out
         sums[t, :, :SPAN] = sums[t, :, :SPAN] + gathered
-        return carry
+      return carry
 
     lax.fori_loop(0, (live_count + (UNROLL - 1)) // UNROLL, some_boards, 0)
 
@@ -267,15 +265,10 @@
         node = worth[a] * mean
         one_share = node if one_share is None else one_share + node
     one_share = jnp.sum(one_share, axis=0, keepdims=True) / (TURNS_ALL * 1.0)
-    tiles = WIDTH // 128
-    for a in range(actions + 1):
-        row = zero[a : a + 1, :] if a < actions else one_share
-        for part in range(tiles):
-            ends = min((part + 1) * 128, HANDS)
-            line = a * tiles + part
-            lines[line : line + 1, 0 : ends - part * 128] = row[:, part * 128 : ends]
+    rows = jnp.concatenate([zero, one_share], axis=0)
     for device in range(message.shape[0]):
-        message[device] = lines[...]
+        for pair in range((actions + 1) // 2):
+            message[device, pair] = rows[2 * pair : 2 * pair + 2, :]
 
 
 def iterate(flop_cards, turn_cards, river_cards, board_count, stakes, reach, flop_reg, turn_reg, ranks):
@@ -301,7 +294,7 @@
         iteration_kernel,
         out_shape=(
             jax.ShapeDtypeStruct((actions, turns, hands), jnp.float32),
-            jax.ShapeDtypeStruct((DEVICES, LINES, 128), jnp.float32),
+            jax.ShapeDtypeStruct((DEVICES, (actions + 1) // 2, 2, hands), jnp.float32),
         ),
         in_specs=[pl.BlockSpec(memory_space=pltpu.HBM)] * len(operands),
         out_specs=(vmem, vmem),
@@ -317,7 +310,6 @@
             pltpu.VMEM((actions, turns, hands), jnp.float32),
             pltpu.VMEM((turns, 16, WIDTH), jnp.float32),
             pltpu.VMEM((2 * turns, WIDTH), jnp.float32),
-            pltpu.VMEM((LINES, 128), jnp.float32),
             pltpu.SemaphoreType.DMA((len(operands),)),
         ],
         compiler_params=pltpu.CompilerParams(vmem_limit_bytes=62 * 1024 * 1024),
@@ -360,12 +352,6 @@
     spread = jnp.broadcast_to(block[None], (count,) + block.shape)
     heard = lax.all_to_all(spread, axis, 0, 0, axis_index_groups=groups, tiled=True)
     return jnp.sum(heard, axis=0)
-
-
-def tiled(rows):
-    count = rows.size
-    padded = -(-count // 1024) * 1024
-    return jnp.pad(rows.reshape(-1), (0, padded - count)).reshape(-1, 128)
 
 
 def per_device(
@@ -397,12 +383,11 @@
         hand_ranks.reshape(turns * rivers, hands),
     )
     heard = lax.all_to_all(message, "turn", 0, 0, tiled=True)
-    heard = jnp.sum(heard, axis=0)[: (actions + 1) * (WIDTH // 128)]
-    total = heard.reshape(actions + 1, WIDTH)[:, :hands]
+    total = jnp.sum(heard, axis=0).reshape(actions + 1, hands)
     regrets = flop_regrets[0]
     flop_policy = regrets / jnp.sum(regrets, axis=0, keepdims=True)
     zero_flop = jnp.sum(flop_policy * total[:actions], axis=0)
-    values = tiled(jnp.stack([zero_flop, total[actions]]))
+    values = jnp.stack([zero_flop, total[actions]])
     flops = lax.axis_size("flop")
     near = [list(range(i, i + 4)) for i in range(0, flops, 4)]
     far = [list(range(i, flops, 4)) for i in range(4)]
@@ -412,8 +397,7 @@
     turn_next = jnp.transpose(turn_new, (0, 2, 1, 3))[None]
     flop_next = jnp.maximum(regrets + total[:actions] - zero_flop, 0.0)[None]
     values = summed(values, "flop", far)
-    root_values = values.reshape(-1)[: 2 * hands].reshape(2, hands)
-    return (flop_next, turn_next, root_values)
+    return (flop_next, turn_next, values)
 
 
 def solution(mesh):

time: 70.1 us -> 69.6 us (level)
  waiting for transfers between devices: 19.5 us -> 18.6 us
  blocking collectives: 8.85 us -> 9.6 us
  other arithmetic: 0.14 us -> 0.87 us
  local copies, waits for them, and re-layouts: 2.12 us -> 1.4 us
    all_to_all x1, blocking collectives: 8.85 us -> 9.6 us  [summed(): lax.all_to_all(spread, axis, 0, 0, axis_index_groups=groups, tiled=True)]
    reshape x3 -> x1, local copies, waits for them, and re-layouts: 0.77 us -> 0.03 us  [per_device(): total = jnp.sum(heard, axis=0).reshape(actions + 1, hands)]
where the time goes in v3:
time: 69.6 us; the launch traced here: 69.2 us
  starting transfers between devices  19.7 us (28%)
  waiting for transfers between devices  18.6 us (27%)
  Pallas kernels  17.7 us (25%)
  blocking collectives  9.6 us (14%)
  local copies, waits for them, and re-layouts  1.4 us (2%)
  between operations  1.36 us (2%)
  other arithmetic  0.87 us (1%)
    pallas_call x1, Pallas kernels, iterate(): pl.pallas_call(iteration_kernel, out_shape=(jax.ShapeDtypeStruct((actions...  15.6 us
    all_to_all x1, starting transfers between devices, summed(): lax.all_to_all(spread, axis, 0, 0, axis_index_groups=groups, tiled=True)  15.4 us
    all_to_all x1, waiting for transfers between devices, summed(): lax.all_to_all(spread, axis, 0, 0, axis_index_groups=groups, tiled=True)  11 us
    all_to_all x1, blocking collectives, summed(): lax.all_to_all(spread, axis, 0, 0, axis_index_groups=groups, tiled=True)  9.6 us
    all_to_all x1, waiting for transfers between devices, per_device(): heard = lax.all_to_all(message, 'turn', 0, 0, tiled=True)  7.58 us
    all_to_all x1, starting transfers between devices, per_device(): heard = lax.all_to_all(message, 'turn', 0, 0, tiled=True)  4.31 us
    pallas_call x1, Pallas kernels, updated(): pl.pallas_call(regret_kernel, out_shape=jax.ShapeDtypeStruct(turn_reg.sha...  2.1 us
  transfers between devices with their start and end apart: 2, of which 2 were waited for; matrix products, arithmetic and copies ran while one was open for 1% of the time, Pallas kernels for 3%

profile of v3, /device:TPU:32, one launch (start us, length us, event | category | flops | bytes accessed | tf_op | source)
XLA Modules:
  0.0 69.2 jit_solution(795185488711345393)
XLA Ops:
  1.3 0.0 copy-start
  1.3 15.6 %iteration.1 = (f32[5,4,1326]{2,1,0:T(4,128)}, f32[8,3,2,1326]{3,2,1,0:T(2,128)}) custom-call(s32[1,3]{1,0:T(1,128)} %flop_cards_hbm.1, s32[1,4]{1,0:T(1,128)} %turn_cards_hbm.1, s32[4,8]{1,0:T(4,128)} %bitcast.23, s32[1,1]{1,0:T(1,128)S(6)} %copy.27.board_count_hbm, f32[5,5]{1,0:T(8,128)} %stakes.1, s32[2,1408]{1,0:T(2,128)} %constant.2.clone.cards_hbm, ...), custom_call_target="tpu_custom_call" | custom-call | flops 1800474624 | bytes 5000000 | tf_op jit(solution)/shard_map/iteration/pallas_call | solution.py:293
  16.9 4.3 %all-to-all-start = ((f32[8,3,2,1326]{3,2,1,0:T(2,128)}), f32[8,3,2,1326]{3,2,1,0:T(2,128)S(1)}, u32[]{:S(2)}, u32[]{:S(2)}) async-start(f32[8,3,2,1326]{3,2,1,0:T(2,128)} %get-tuple-element.9), calls=%async_computation | async-start | bytes 540672 | tf_op jit(solution)/shard_map/all_to_all | solution.py:385
  21.2 0.0 copy-done
  21.3 7.6 %all-to-all-done = f32[8,3,2,1326]{3,2,1,0:T(2,128)S(1)} async-done(((f32[8,3,2,1326]{3,2,1,0:T(2,128)}), f32[8,3,2,1326]{3,2,1,0:T(2,128)S(1)}, u32[]{:S(2)}, u32[]{:S(2)}) %all-to-all-start) | async-done | bytes 254624 | tf_op jit(solution)/shard_map/all_to_all | solution.py:385
  28.9 0.1 reduce_sum.46
  29.1 9.6 %all_to_all.15 = f32[4,2,1326]{2,1,0:T(2,128)S(1)} all-to-all(f32[4,2,1326]{2,1,0:T(2,128)S(1)} %broadcast_in_dim.8), channel_id=1, replica_groups={{0,8,16,24},{32,40,48,56},{64,72,80,88},{96,104,112,120},{128,136,144,1..., dimensions={0} | all-to-all | bytes 84864 | tf_op jit(solution)/shard_map/all_to_all | solution.py:353
  38.7 0.7 %broadcast_in_dim.11 = f32[16,2,1326]{2,1,0:T(2,128)} broadcast(f32[2,1326]{1,0:T(2,128)S(1)} %reduce_sum.48), dimensions={1,2} | broadcast | bytes 180336 | tf_op jit(solution)/shard_map/broadcast_in_dim | solution.py:352
  39.4 15.4 %all-to-all-start.2 = ((f32[16,2,1326]{2,1,0:T(2,128)}), f32[16,2,1326]{2,1,0:T(2,128)S(1)}, u32[]{:S(2)}, u32[]{:S(2)}) async-start(f32[16,2,1326]{2,1,0:T(2,128)} %broadcast_in_dim.11), calls=%async_computation.2 | async-start | bytes 360448 | tf_op jit(solution)/shard_map/all_to_all | solution.py:353
  54.8 0.6 broadcast_in_dim.9
  55.5 2.1 %turn_regrets.1 = f32[5,5,4,1326]{3,2,1,0:T(4,128)} custom-call(f32[5,5]{1,0:T(8,128)} %stakes.1, f32[5,4,1326]{2,1,0:T(4,128)} %get-tuple-element.13.mean, f32[5,5,4,1326]{3,2,1,0:T(4,128)} %bitcast.19), custom_call_target="tpu_custom_call" | custom-call | flops 2000000 | bytes 1200000 | tf_op jit(solution)/shard_map/turn_regrets/pallas_call | solution.py:340
  57.6 11.0 %all-to-all-done.2 = f32[16,2,1326]{2,1,0:T(2,128)S(1)} async-done(((f32[16,2,1326]{2,1,0:T(2,128)}), f32[16,2,1326]{2,1,0:T(2,128)S(1)}, u32[]{:S(2)}, u32[]{:S(2)}) %all-to-all-start.2) | async-done | bytes 169760 | tf_op jit(solution)/shard_map/all_to_all | solution.py:353
  68.6 0.7 reduce_sum.49
  (9 shorter events, 0.2 us)
Async XLA Ops:
  1.3 20.0 %copy-start = (f32[1,5,1326]{2,0,1:T(1,128)S(1)}, f32[1,5,1326]{2,0,1:T(1,128)}, u32[]{:S(2)}) copy-start(f32[1,5,1326]{2,0,1:T(1,128)} %param.13) | copy-start | bytes 79564
  16.9 11.9 %all-to-all-start = ((f32[8,3,2,1326]{3,2,1,0:T(2,128)}), f32[8,3,2,1326]{3,2,1,0:T(2,128)S(1)}, u32[]{:S(2)}, u32[]{:S(2)}) async-start(f32[8,3,2,1326]{3,2,1,0:T(2,128)} %get-tuple-element.9), calls=%async_computation | async-start | bytes 540672 | tf_op jit(solution)/shard_map/all_to_all | solution.py:385
  39.4 29.1 %all-to-all-start.2 = ((f32[16,2,1326]{2,1,0:T(2,128)}), f32[16,2,1326]{2,1,0:T(2,128)S(1)}, u32[]{:S(2)}, u32[]{:S(2)}) async-start(f32[16,2,1326]{2,1,0:T(2,128)} %broadcast_in_dim.11), calls=%async_computation.2 | async-start | bytes 360448 | tf_op jit(solution)/shard_map/all_to_all | solution.py:353

commit v4 on v3

--- a/solution.py
+++ b/solution.py
@@ -14,7 +14,7 @@
 SPAN = 1152
 SHIFTS = 8
 CHUNK = 256
-UNROLL = 16
+UNROLL = 32
 TURNS_ALL = 32
 DEVICES = 8
 

time: 69.6 us -> 69.4 us (level)
  no operation moved by 1% of the time
where the time goes in v4:
time: 69.4 us; the launch traced here: 69 us
  starting transfers between devices  19.5 us (28%)
  waiting for transfers between devices  18.6 us (27%)
  Pallas kernels  17.5 us (25%)
  blocking collectives  9.78 us (14%)
  local copies, waits for them, and re-layouts  1.4 us (2%)
  between operations  1.36 us (2%)
  other arithmetic  0.87 us (1%)
    pallas_call x1, Pallas kernels, iterate(): pl.pallas_call(iteration_kernel, out_shape=(jax.ShapeDtypeStruct((actions...  15.4 us
    all_to_all x1, starting transfers between devices, summed(): lax.all_to_all(spread, axis, 0, 0, axis_index_groups=groups, tiled=True)  15.2 us
    all_to_all x1, waiting for transfers between devices, summed(): lax.all_to_all(spread, axis, 0, 0, axis_index_groups=groups, tiled=True)  11 us
    all_to_all x1, blocking collectives, summed(): lax.all_to_all(spread, axis, 0, 0, axis_index_groups=groups, tiled=True)  9.78 us
    all_to_all x1, waiting for transfers between devices, per_device(): heard = lax.all_to_all(message, 'turn', 0, 0, tiled=True)  7.58 us
    all_to_all x1, starting transfers between devices, per_device(): heard = lax.all_to_all(message, 'turn', 0, 0, tiled=True)  4.31 us
    pallas_call x1, Pallas kernels, updated(): pl.pallas_call(regret_kernel, out_shape=jax.ShapeDtypeStruct(turn_reg.sha...  2.1 us
  transfers between devices with their start and end apart: 2, of which 2 were waited for; matrix products, arithmetic and copies ran while one was open for 1% of the time, Pallas kernels for 3%

profile of v4, /device:TPU:32, one launch (start us, length us, event | category | flops | bytes accessed | tf_op | source)
XLA Modules:
  0.0 69.0 jit_solution(9641670069631587394)
XLA Ops:
  1.3 0.0 copy-start
  1.3 15.4 %iteration.1 = (f32[5,4,1326]{2,1,0:T(4,128)}, f32[8,3,2,1326]{3,2,1,0:T(2,128)}) custom-call(s32[1,3]{1,0:T(1,128)} %flop_cards_hbm.1, s32[1,4]{1,0:T(1,128)} %turn_cards_hbm.1, s32[4,8]{1,0:T(4,128)} %bitcast.23, s32[1,1]{1,0:T(1,128)S(6)} %copy.27.board_count_hbm, f32[5,5]{1,0:T(8,128)} %stakes.1, s32[2,1408]{1,0:T(2,128)} %constant.2.clone.cards_hbm, ...), custom_call_target="tpu_custom_call" | custom-call | flops 1800474624 | bytes 5000000 | tf_op jit(solution)/shard_map/iteration/pallas_call | solution.py:293
  16.7 4.3 %all-to-all-start = ((f32[8,3,2,1326]{3,2,1,0:T(2,128)}), f32[8,3,2,1326]{3,2,1,0:T(2,128)S(1)}, u32[]{:S(2)}, u32[]{:S(2)}) async-start(f32[8,3,2,1326]{3,2,1,0:T(2,128)} %get-tuple-element.9), calls=%async_computation | async-start | bytes 540672 | tf_op jit(solution)/shard_map/all_to_all | solution.py:385
  21.0 0.0 copy-done
  21.1 7.6 %all-to-all-done = f32[8,3,2,1326]{3,2,1,0:T(2,128)S(1)} async-done(((f32[8,3,2,1326]{3,2,1,0:T(2,128)}), f32[8,3,2,1326]{3,2,1,0:T(2,128)S(1)}, u32[]{:S(2)}, u32[]{:S(2)}) %all-to-all-start) | async-done | bytes 254624 | tf_op jit(solution)/shard_map/all_to_all | solution.py:385
  28.7 0.1 reduce_sum.46
  28.9 9.8 %all_to_all.15 = f32[4,2,1326]{2,1,0:T(2,128)S(1)} all-to-all(f32[4,2,1326]{2,1,0:T(2,128)S(1)} %broadcast_in_dim.8), channel_id=1, replica_groups={{0,8,16,24},{32,40,48,56},{64,72,80,88},{96,104,112,120},{128,136,144,1..., dimensions={0} | all-to-all | bytes 84864 | tf_op jit(solution)/shard_map/all_to_all | solution.py:353
  38.7 0.7 %broadcast_in_dim.11 = f32[16,2,1326]{2,1,0:T(2,128)} broadcast(f32[2,1326]{1,0:T(2,128)S(1)} %reduce_sum.48), dimensions={1,2} | broadcast | bytes 180336 | tf_op jit(solution)/shard_map/broadcast_in_dim | solution.py:352
  39.4 15.2 %all-to-all-start.2 = ((f32[16,2,1326]{2,1,0:T(2,128)}), f32[16,2,1326]{2,1,0:T(2,128)S(1)}, u32[]{:S(2)}, u32[]{:S(2)}) async-start(f32[16,2,1326]{2,1,0:T(2,128)} %broadcast_in_dim.11), calls=%async_computation.2 | async-start | bytes 360448 | tf_op jit(solution)/shard_map/all_to_all | solution.py:353
  54.7 0.6 broadcast_in_dim.9
  55.3 2.1 %turn_regrets.1 = f32[5,5,4,1326]{3,2,1,0:T(4,128)} custom-call(f32[5,5]{1,0:T(8,128)} %stakes.1, f32[5,4,1326]{2,1,0:T(4,128)} %get-tuple-element.13.mean, f32[5,5,4,1326]{3,2,1,0:T(4,128)} %bitcast.19), custom_call_target="tpu_custom_call" | custom-call | flops 2000000 | bytes 1200000 | tf_op jit(solution)/shard_map/turn_regrets/pallas_call | solution.py:340
  57.4 11.0 %all-to-all-done.2 = f32[16,2,1326]{2,1,0:T(2,128)S(1)} async-done(((f32[16,2,1326]{2,1,0:T(2,128)}), f32[16,2,1326]{2,1,0:T(2,128)S(1)}, u32[]{:S(2)}, u32[]{:S(2)}) %all-to-all-start.2) | async-done | bytes 169760 | tf_op jit(solution)/shard_map/all_to_all | solution.py:353
  68.4 0.7 reduce_sum.49
  (9 shorter events, 0.2 us)
Async XLA Ops:
  1.3 19.8 %copy-start = (f32[1,5,1326]{2,0,1:T(1,128)S(1)}, f32[1,5,1326]{2,0,1:T(1,128)}, u32[]{:S(2)}) copy-start(f32[1,5,1326]{2,0,1:T(1,128)} %param.13) | copy-start | bytes 79564
  16.7 11.9 %all-to-all-start = ((f32[8,3,2,1326]{3,2,1,0:T(2,128)}), f32[8,3,2,1326]{3,2,1,0:T(2,128)S(1)}, u32[]{:S(2)}, u32[]{:S(2)}) async-start(f32[8,3,2,1326]{3,2,1,0:T(2,128)} %get-tuple-element.9), calls=%async_computation | async-start | bytes 540672 | tf_op jit(solution)/shard_map/all_to_all | solution.py:385
  39.4 28.9 %all-to-all-start.2 = ((f32[16,2,1326]{2,1,0:T(2,128)}), f32[16,2,1326]{2,1,0:T(2,128)S(1)}, u32[]{:S(2)}, u32[]{:S(2)}) async-start(f32[16,2,1326]{2,1,0:T(2,128)} %broadcast_in_dim.11), calls=%async_computation.2 | async-start | bytes 360448 | tf_op jit(solution)/shard_map/all_to_all | solution.py:353
